TPU v7x, 256 devices: a whole 4x4x8 slice. The times are simulated.
256 devices in a mesh: space: 64 (over z, y_lo, x), chan: 4 (over y_hi, core).
Axes of the slice: x: 4, y: 4 (y_hi: 2, y_lo: 2; y = y_hi * 2 + y_lo), z: 8, core: 2. Of those that a mesh axis runs over, the one named last changes fastest.
Arguments:
- features: bfloat16 [4096, 32, 512], P(('space', 'chan')), may hold values from -6 to 6
- occupancy: int32 [4096], P(('space', 'chan')), may hold values 0 or 1
- neighbours: int32 [4096, 6], P(('space', 'chan')), may hold values from -1 to 4095, as said below
- conv_weight: bfloat16 [27, 32, 32], replicated, may hold values from -0.21875 to 0.21875
- conv_bias: float32 [32], replicated, may hold values from -3 to 3
- latent: bfloat16 [262144, 512], P(('space', 'chan')), may hold values from -6 to 6
- token_proj: bfloat16 [32, 512], replicated, may hold values from -1 to 1
- norm_gain: float32 [512], replicated, may hold values from 0.25 to 1.75
- qkv_weight: bfloat16 [3, 512, 512], replicated
- out_weight: bfloat16 [512, 512], replicated, may hold values from -0.25 to 0.25
Outputs:
- conv_out: bfloat16 [4096, 32, 512], P(('space', 'chan'))
- tokens_out: bfloat16 [512, 262144], P(None, ('space', 'chan'))
Inputs may be any that keep to these rules, and one draw needn't show every extreme that they name: `neighbours`: entry [b, d] is the brick across face d of brick b (d = 0..5 for -x, +x, -y, +y, -z, +z), or -1 where there is none. Brick b lies on device b // 16 in the order of space+chan, and a neighbour lies on a device whose index differs from its brick's by at most 2.
All inputs are finite; a program needn't handle non-finite values. No bound on the sum of `occupancy` on one device may be relied on, other than what follows from the above.
Results may differ from a plain program's by a relative error of at most 0.0054.
Values may be sent and summed in bfloat16 or wider, within the bound.
A program may use at most 128 MiB of HBM per device.

v0:
```python
import math

import jax
import jax.numpy as jnp
import numpy as np
from jax import lax
from jax.sharding import PartitionSpec as P

HD = 64
WIN = 1024
REACH = 2


def passed_along(value, axis, steps):
    count = lax.axis_size(axis)
    first, last = (max(0, -steps), min(count, count - steps))
    return lax.ppermute(value, axis, [(source, source + steps) for source in range(first, last)])


def shifted(array, axis, by):
    size = lax.axis_size(axis)
    return lax.ppermute(array, axis, [(i, (i + by) % size) for i in range(size)])


def sheet_sources():
    table = np.zeros((6, 64), np.int64)
    cells = np.arange(64)
    high, low = (cells // 8, cells % 8)
    table[0] = 448 + cells
    table[1] = cells
    table[2] = 64 * high + 56 + low
    table[3] = 64 * high + low
    table[4] = 64 * high + 8 * low + 7
    table[5] = 64 * high + 8 * low
    return table


def take_table():
    sources = sheet_sources()
    table = np.zeros((512, 6, 64), np.float32)
    for face in range(6):
        table[sources[face], face, np.arange(64)] = 1.0
    return jnp.asarray(table, jnp.bfloat16)


def place_table():
    sources = sheet_sources()
    table = np.zeros((6, 64, 512), np.float32)
    for face in range(6):
        table[face, np.arange(64), sources[face ^ 1]] = 1.0
    return jnp.asarray(table.reshape(3, 2, 64, 512), jnp.bfloat16)


def pool_table():
    table = np.zeros((512, 64), np.float32)
    for voxel in range(512):
        pos_x, pos_y, pos_z = (voxel // 64, voxel // 8 % 8, voxel % 8)
        cell_p, cell_q, cell_r = (pos_x // 2, pos_y // 2, pos_z // 2)
        target = (
            32 * (cell_p // 2)
            + 16 * (cell_q // 2)
            + 8 * (cell_r // 2)
            + 4 * (cell_p % 2)
            + 2 * (cell_q % 2)
            + cell_r % 2
        )
        table[voxel, target] = 0.125
    return jnp.asarray(table, jnp.bfloat16)


def shift_lanes(source, offset):
    if offset == 0:
        return source
    zero_shape = source.shape[:-1] + (abs(offset),)
    filler = jnp.zeros(zero_shape, source.dtype)
    if offset > 0:
        return jnp.concatenate([source[..., offset:], filler], axis=-1)
    return jnp.concatenate([filler, source[..., :offset]], axis=-1)


def inside(coord, step):
    return (coord + step >= 0) & (coord + step < 8)


def tap_inputs(vox, ghosts):
    lanes = jnp.arange(512, dtype=jnp.int32)
    coords = (lanes // 64, lanes // 8 % 8, lanes % 8)
    strides = (64, 8, 1)
    tap_list = []
    for step_x in (-1, 0, 1):
        for step_y in (-1, 0, 1):
            for step_z in (-1, 0, 1):
                steps_now = (step_x, step_y, step_z)
                offset = 64 * step_x + 8 * step_y + step_z
                within = (
                    inside(coords[0], step_x)
                    & inside(coords[1], step_y)
                    & inside(coords[2], step_z)
                )
                total = shift_lanes(vox, offset) * within.astype(vox.dtype)
                for axis_id in range(3):
                    if steps_now[axis_id] != 0:
                        others = [
                            inside(coords[other], steps_now[other])
                            for other in range(3)
                            if other != axis_id
                        ]
                        outside = (
                            jnp.logical_not(inside(coords[axis_id], steps_now[axis_id]))
                            & others[0]
                            & others[1]
                        )
                        ghost_shift = shift_lanes(
                            ghosts[:, axis_id], offset - steps_now[axis_id] * strides[axis_id]
                        )
                        total = total + ghost_shift * outside.astype(vox.dtype)
                tap_list.append(total)
    return jnp.stack(tap_list, axis=1)


def convolve(vox, ghosts, weight):
    brick_count, channels = (vox.shape[0], vox.shape[1])
    out_channels = weight.shape[1]
    group_size = math.gcd(brick_count, 8)
    flat_weight = weight.transpose(1, 0, 2).reshape(out_channels, 27 * channels)

    def per_group(inputs):
        vox_group, ghost_group = inputs
        patches = tap_inputs(vox_group, ghost_group).reshape(group_size, 27 * channels, 512)
        return jnp.einsum("ok,bkv->bov", flat_weight, patches, preferred_element_type=jnp.float32)

    grouped_vox = vox.reshape(brick_count // group_size, group_size, channels, 512)
    grouped_ghost = ghosts.reshape(brick_count // group_size, group_size, 3, channels, 512)
    summed = lax.map(per_group, (grouped_vox, grouped_ghost))
    return summed.reshape(brick_count, out_channels, 512)


def rms_norm(mixed_in, norm_gain):
    scale_row = lax.rsqrt(jnp.mean(mixed_in * mixed_in, axis=-1, keepdims=True) + 1e-06)
    return (mixed_in * scale_row * norm_gain[None, :]).astype(jnp.bfloat16)


def attend_windows(query_ext, kv_ext, alive_ext):
    feat_count, length = query_ext.shape
    count = length // WIN
    head_count = feat_count // HD
    diagonal = jnp.eye(WIN, dtype=bool)

    def per_window(index, result):
        start = index * WIN
        query_heads = lax.dynamic_slice_in_dim(query_ext, start, WIN, 1).reshape(
            head_count, HD, WIN
        )
        kv_block = lax.dynamic_slice_in_dim(kv_ext, start, WIN, 2)
        alive_block = lax.dynamic_slice_in_dim(alive_ext, start, WIN, 0)
        key_heads = kv_block[0].reshape(head_count, HD, WIN)
        value_heads = kv_block[1].reshape(head_count, HD, WIN)
        scores = jnp.einsum(
            "hdq,hdk->hqk", query_heads, key_heads, preferred_element_type=jnp.float32
        ) * HD ** (-0.5)
        allowed = (alive_block[None, None, :] > 0) | diagonal[None]
        row_peak = jnp.max(jnp.where(allowed, scores, -1e30), axis=-1, keepdims=True)
        raw = jnp.where(allowed, jnp.exp(scores - row_peak), 0.0)
        weights_bf = (raw / jnp.sum(raw, axis=-1, keepdims=True)).astype(jnp.bfloat16)
        output = jnp.einsum(
            "hqk,hdk->hdq", weights_bf, value_heads, preferred_element_type=jnp.float32
        )
        output = output.astype(jnp.bfloat16).reshape(feat_count, WIN)
        return lax.dynamic_update_slice_in_dim(result, output, start, 1)

    empty = jnp.zeros((feat_count, length), jnp.bfloat16)
    return lax.fori_loop(0, count, per_window, empty)


def local(
    features,
    occupancy,
    neighbours,
    conv_weight,
    conv_bias,
    latent,
    token_proj,
    norm_gain,
    qkv_weight,
    out_weight,
):
    my_index = lax.axis_index(("space", "chan"))
    brick_count, channels = (features.shape[0], features.shape[1])
    alive_bf = occupancy.astype(jnp.bfloat16)
    masked = features * alive_bf[:, None, None]
    has_peer = neighbours >= 0
    peer_index = jnp.where(has_peer, neighbours, 0)
    source = jnp.clip(peer_index // brick_count - my_index, -REACH, REACH)
    face_row = ((source + REACH) * brick_count + peer_index % brick_count) * 6 + jnp.arange(
        6, dtype=jnp.int32
    )[None, :]
    own_faces = jnp.einsum(
        "bcv,vfk->bfck", masked, take_table(), preferred_element_type=jnp.float32
    )
    own_faces = own_faces.astype(jnp.bfloat16).reshape(brick_count, 6, channels * 64)
    received = {0: own_faces}
    for spread in range(-REACH, REACH + 1):
        if spread != 0:
            received[spread] = passed_along(own_faces, ("space", "chan"), -spread)
    face_store = jnp.concatenate([received[spread] for spread in range(-REACH, REACH + 1)], axis=0)
    face_store = face_store.reshape(-1, channels * 64)
    picked = jnp.take(face_store, face_row.reshape(-1), axis=0).reshape(
        brick_count, 6, channels * 64
    )
    gathered = jnp.where(has_peer[:, :, None], picked, jnp.zeros_like(picked))
    sheets = gathered.reshape(brick_count, 3, 2, channels, 64)
    ghosts = jnp.einsum(
        "bgsck,gskv->bgcv", sheets, place_table(), preferred_element_type=jnp.float32
    ).astype(jnp.bfloat16)
    summed = convolve(masked, ghosts, conv_weight)
    alive_f = occupancy.astype(jnp.float32)
    mixed = masked.astype(jnp.float32) + jax.nn.silu(summed + conv_bias[None, :, None])
    conv_out = (alive_f[:, None, None] * mixed).astype(jnp.bfloat16)
    pooled = jnp.einsum(
        "bcv,vm->bcm", conv_out, pool_table(), preferred_element_type=jnp.float32
    ).astype(jnp.bfloat16)
    lifted = jnp.einsum("bcm,cd->bmd", pooled, token_proj, preferred_element_type=jnp.float32)
    mixed_in = latent.astype(jnp.float32) + lifted.reshape(brick_count * 64, token_proj.shape[1])
    normed = rms_norm(mixed_in, norm_gain)
    projected = lax.dot_general(
        qkv_weight, normed, (((1,), (1,)), ((), ())), preferred_element_type=jnp.float32
    ).astype(jnp.bfloat16)
    tok_count = projected.shape[2]
    token_alive = jnp.broadcast_to(occupancy[:, None], (brick_count, 64)).reshape(tok_count)
    half_win = WIN // 2
    kv_part = projected[1:3]
    before_kv, before_alive = shifted(
        (kv_part[:, :, tok_count - half_win :], token_alive[tok_count - half_win :]),
        ("space", "chan"),
        1,
    )
    after_kv, after_alive = shifted(
        (kv_part[:, :, :half_win], token_alive[:half_win]), ("space", "chan"), -1
    )
    kv_ext = jnp.concatenate([before_kv, kv_part, after_kv], axis=2)
    alive_ext = jnp.concatenate([before_alive, token_alive, after_alive], axis=0)
    query_ext = jnp.pad(projected[0], ((0, 0), (half_win, half_win)))
    attended = attend_windows(query_ext, kv_ext, alive_ext)[:, half_win : half_win + tok_count]
    mixing = lax.dot_general(
        out_weight, attended, (((0,), (0,)), ((), ())), preferred_element_type=jnp.float32
    )
    tokens_out = (mixed_in.T + mixing).astype(jnp.bfloat16)
    return (conv_out, tokens_out)


def solution(mesh):
    return jax.shard_map(
        local,
        mesh=mesh,
        in_specs=(
            P(("space", "chan"), None, None),
            P(("space", "chan")),
            P(("space", "chan"), None),
            P(),
            P(),
            P(("space", "chan"), None),
            P(),
            P(),
            P(),
            P(),
        ),
        out_specs=(P(("space", "chan"), None, None), P(None, ("space", "chan"))),
        check_vma=False,
    )
```

profile of v0, /device:TPU:1, one launch (start us, length us, event | category | flops | bytes accessed | tf_op | source)
XLA Modules:
  0.0 216.6 jit_solution(15791629677778607790)
XLA Ops:
  1.4 1.1 broadcast_multiply_fusion
  2.6 1.6 fusion.68
  5.0 1.3 collective-permute-start.3
  6.3 5.2 %collective-permute-start.2 = (bf16[16,6,2048]{2,0,1:T(8,128)(2,1)S(1)}, bf16[16,6,2048]{2,0,1:T(8,128)(2,1)}, u32[]{:S(2)}, u32[]{:S(2)}) collective-permute-start(bf16[16,6,2048]{2,0,1:T(8,128)(2,1)S(1)} %copy.91), channel_id=1, source_target_pairs={{1,0},{2,1},{3,2},{4,3},{5,4},{6,5},{7,6},{8,7},{9,8},{10,9},{11,1... | collective-permute-start | bytes 1179656 | tf_op jit(solution)/shard_map/ppermute | solution.py:17
  11.5 5.7 %collective-permute-start.1 = (bf16[16,6,2048]{2,0,1:T(8,128)(2,1)S(1)}, bf16[16,6,2048]{2,0,1:T(8,128)(2,1)}, u32[]{:S(2)}, u32[]{:S(2)}) collective-permute-start(bf16[16,6,2048]{2,0,1:T(8,128)(2,1)S(1)} %copy.91), channel_id=1, source_target_pairs={{0,1},{1,2},{2,3},{3,4},{4,5},{5,6},{6,7},{7,8},{8,9},{9,10},{10,1... | collective-permute-start | bytes 1179656 | tf_op jit(solution)/shard_map/ppermute | solution.py:17
  17.2 4.7 %collective-permute-start = (bf16[16,6,2048]{2,0,1:T(8,128)(2,1)S(1)}, bf16[16,6,2048]{2,0,1:T(8,128)(2,1)}, u32[]{:S(2)}, u32[]{:S(2)}) collective-permute-start(bf16[16,6,2048]{2,0,1:T(8,128)(2,1)S(1)} %copy.91), channel_id=1, source_target_pairs={{0,2},{1,3},{2,4},{3,5},{4,6},{5,7},{6,8},{7,9},{8,10},{9,11},{10,... | collective-permute-start | bytes 1179656 | tf_op jit(solution)/shard_map/ppermute | solution.py:17
  23.8 1.0 copy.82
  25.1 12.3 %collective-permute-done = bf16[16,6,2048]{2,0,1:T(8,128)(2,1)} collective-permute-done((bf16[16,6,2048]{2,0,1:T(8,128)(2,1)S(1)}, bf16[16,6,2048]{2,0,1:T(8,128)(2,1)}, u32[]{:S(2)}, u32[]{:S(2)}) %collective-permute-start) | collective-permute-done | bytes 393248 | tf_op jit(solution)/shard_map/ppermute | solution.py:17
  39.7 1.0 constant_dynamic-update-slice_fusion.2
  40.7 1.0 constant_dynamic-update-slice_fusion.1
  41.7 2.6 %copy.79 = bf16[80,6,2048]{2,1,0:T(8,128)(2,1)} copy(bf16[80,6,2048]{2,0,1:T(8,128)(2,1)S(1)} %constant_dynamic-update-slice_fusion.1) | data formatting | bytes 3932160 | tf_op jit(solution)/shard_map/concatenate | solution.py:205
  44.3 4.2 %reshape.582 = bf16[480,2048]{1,0:T(8,128)(2,1)} reshape(bf16[80,6,2048]{2,1,0:T(8,128)(2,1)} %copy.79) | data formatting | bytes 3932160 | tf_op jit(solution)/shard_map/reshape | solution.py:206
  48.5 3.0 %gather_fusion = bf16[96,2048]{1,0:T(8,128)(2,1)S(1)} fusion(bf16[480,2048]{1,0:T(8,128)(2,1)} %reshape.582, s32[1024]{0:T(1024)S(1)} %pad_clamp_fusion), kind=kCustom, calls=%fused_computation | custom fusion | bytes 786816 | tf_op jit(solution)/shard_map/jit(_take)/gather | solution.py:207
  52.3 3.2 %bitcast_convert_fusion = bf16[3,16,32,512]{3,2,1,0:T(8,128)(2,1)} fusion(bf16[3,2,64,512,1]{3,2,1,4,0:T(8,128)(2,1)} %constant.690, bf16[16,3,2,32,64]{4,3,2,1,0:T(8,128)(2,1)S(1)} %gather.7, pred[16,3,2]{2,0,1:T(8,128)(4,1)S(1)} %copy.77, pred[16,3,2]{2,0,1:T(8,128)(4,1)S(1)} %copy.76), kind=kOutput, calls=%fused_computation.206 | convolution fusion | flops 202506240 | bytes 2359488 | tf_op jit(solution)/shard_map/bgsck,gskv->bgcv/dot_general | solution.py:212
  55.5 29.6 %while.27 = (s32[]{:T(128)}, f32[2,8,32,512]{3,2,1,0:T(8,128)}, bf16[2,8,32,512]{3,2,1,0:T(8,128)(2,1)S(1)}, bf16[2,8,3,32,512]{4,3,1,0,2:T(8,128)(2,1)}, bf16[32,864]{1,0:T(8,128)(2,1)S(1)}, /*index=5*/s32[]{:T(128)}) while((s32[]{:T(128)}, f32[2,8,32,512]{3,2,1,0:T(8,128)}, bf16[2,8,32,512]{3,2,1,0:T(8,128)(2,1)S(1)}, ...), condition=%wide.region_1.2_spmd, body=%wide.region_0.1_spmd.sunk | while | flops 270078464 | bytes 78502576 | solution.py:134
  68.1 1.3 fusion.197
  82.8 1.3 fusion.197
  85.1 1.7 multiply_convert_fusion.1
  86.8 2.3 %fusion.69 = f32[16,64,512]{2,1,0:T(8,128)} fusion(bf16[16,32,512]{2,1,0:T(8,128)(2,1)S(1)} %multiply_convert_fusion.1, bf16[512,64,1]{1,0,2:T(8,128)(2,1)S(1)} %copy-done.13, bf16[32,512]{1,0:T(8,128)(2,1)S(1)} %copy-done.14), kind=kOutput, calls=%fused_computation.216 | convolution fusion | flops 67141632 | bytes 2719744 | tf_op jit(solution)/shard_map/bcm,cd->bmd/dot_general | solution.py:222
  89.1 2.2 %multiply_reduce_fusion = (f32[1024]{0:T(1024)S(1)}, f32[1024,512]{1,0:T(8,128)S(1)}) fusion(f32[16,64,512]{2,1,0:T(8,128)} %fusion.69, bf16[1024,512]{1,0:T(8,128)(2,1)} %param.22), kind=kLoop, calls=%fused_computation.211 | loop fusion | flops 2096128 | bytes 5246976 | tf_op jit(solution)/shard_map/reduce_sum | solution.py:139
  91.3 1.9 convert_bitcast_fusion
  93.2 1.6 copy-done.4
  94.8 1.1 fusion.123
  96.7 4.5 %collective-permute-start.7 = (s32[512]{0:T(512)S(1)}, s32[512]{0:T(512)S(1)}, u32[]{:S(2)}, u32[]{:S(2)}) collective-permute-start(s32[512]{0:T(512)S(1)} %slice.497), channel_id=1, source_target_pairs={{0,255},{1,0},{2,1},{3,2},{4,3},{5,4},{6,5},{7,6},{8,7},{9,8},{10,... | collective-permute-start | bytes 6152 | tf_op jit(solution)/shard_map/ppermute | solution.py:22
  101.5 22.2 %collective-permute-done.7 = s32[512]{0:T(512)S(1)} collective-permute-done((s32[512]{0:T(512)S(1)}, s32[512]{0:T(512)S(1)}, u32[]{:S(2)}, u32[]{:S(2)}) %collective-permute-start.7) | collective-permute-done | bytes 2080 | tf_op jit(solution)/shard_map/ppermute | solution.py:22
  123.7 1.3 slice_bitcast_fusion.3
  125.0 1.5 pad.254
  126.5 3.4 %pad_maximum_fusion = bf16[2,512,2048]{1,2,0:T(8,128)(2,1)} fusion(bf16[2,512,512]{1,2,0:T(8,128)(2,1)} %collective-permute-done.5, bf16[2,512,1024]{1,2,0:T(8,128)(2,1)S(1)} %slice-done, bf16[2,512,512]{1,2,0:T(8,128)(2,1)} %collective-permute-done.4), kind=kLoop, calls=%fused_computation.205 | loop fusion | flops 12582912 | bytes 8388608 | tf_op jit(solution)/shard_map/concatenate | solution.py:240
  129.9 1.6 broadcast_in_dim.87
  131.5 81.0 %while.28 = (s32[]{:T(128)}, bf16[512,2048]{1,0:T(8,128)(2,1)}, bf16[2,512,2048]{1,2,0:T(8,128)(2,1)}, s32[2048]{0:T(1024)S(1)}, bf16[512,2048]{0,1:T(8,128)(2,1...) while((s32[]{:T(128)}, bf16[512,2048]{1,0:T(8,128)(2,1)}, ...), condition=%wide.region_6.7_spmd.clone, body=%wide.region_3.6_spmd.clone.sunk | while | flops 3290957824 | bytes 109123840 | solution.py:172
  131.5 1.3 fusion.203
  132.8 1.3 constant_dynamic-slice_fusion.6
  134.1 1.3 copy.106
  135.4 1.7 constant_dynamic-slice_fusion.5
  137.1 1.3 copy.105
  138.9 19.1 %fusion.204 = (f32[8,1024]{1,0:T(8,128)S(1)}, f32[8,1024,1024]{1,2,0:T(8,128)}) fusion(pred[1024,1024]{0,1:T(8,128)(4,1)} %fusion.203, bf16[8,64,1024]{2,1,0:T(8,128)(2,1)} %bitcast.304, bf16[8,64,1024]{2,1,0:T(8,128)(2,1)S(1)} %bitcast.306), kind=kOutput, calls=%fused_computation.290.clone.1 | convolution fusion | flops 2197816320 | bytes 36732928 | tf_op jit(solution)/shard_map/while/body/eval_jaxpr/sub | solution.py:163
  158.0 12.5 %fusion.205 = bf16[8,64,1024]{2,1,0:T(8,128)(2,1)S(1)} fusion(bf16[8,64,1024]{2,1,0:T(8,128)(2,1)S(1)} %bitcast.305, f32[8,1024,1024]{1,2,0:T(8,128)} %get-tuple-element.711, f32[8,1024]{1,0:T(8,128)S(1)} %get-tuple-element.712), kind=kOutput, calls=%fused_computation.197.clone.1 | convolution fusion | flops 1091043328 | bytes 35684352 | tf_op jit(solution)/shard_map/while/body/eval_jaxpr/hqk,hdk->hdq/dot_general | solution.py:165
  170.7 1.3 copy-done.7
  172.0 1.3 fusion.203
  173.3 1.3 constant_dynamic-slice_fusion.6
  174.6 1.3 copy.106
  175.9 1.7 constant_dynamic-slice_fusion.5
  177.6 1.3 copy.105
  179.5 19.1 %fusion.204 = (f32[8,1024]{1,0:T(8,128)S(1)}, f32[8,1024,1024]{1,2,0:T(8,128)}) fusion(pred[1024,1024]{0,1:T(8,128)(4,1)} %fusion.203, bf16[8,64,1024]{2,1,0:T(8,128)(2,1)} %bitcast.304, bf16[8,64,1024]{2,1,0:T(8,128)(2,1)S(1)} %bitcast.306), kind=kOutput, calls=%fused_computation.290.clone.1 | convolution fusion | flops 2197816320 | bytes 36732928 | tf_op jit(solution)/shard_map/while/body/eval_jaxpr/sub | solution.py:163
  198.6 12.5 %fusion.205 = bf16[8,64,1024]{2,1,0:T(8,128)(2,1)S(1)} fusion(bf16[8,64,1024]{2,1,0:T(8,128)(2,1)S(1)} %bitcast.305, f32[8,1024,1024]{1,2,0:T(8,128)} %get-tuple-element.711, f32[8,1024]{1,0:T(8,128)S(1)} %get-tuple-element.712), kind=kOutput, calls=%fused_computation.197.clone.1 | convolution fusion | flops 1091043328 | bytes 35684352 | tf_op jit(solution)/shard_map/while/body/eval_jaxpr/hqk,hdk->hdq/dot_general | solution.py:165
  211.2 1.3 copy-done.7
  212.5 2.8 %fusion.67 = bf16[512,1024]{0,1:T(8,128)(2,1)S(1)} fusion(f32[1024,512]{1,0:T(8,128)} %copy-done.5, bf16[512,512]{1,0:T(8,128)(2,1)S(1)} %copy-done.12, bf16[512,2048]{1,0:T(8,128)(2,1)} %get-tuple-element.205), kind=kOutput, calls=%fused_computation.213 | convolution fusion | flops 537919488 | bytes 4718592 | tf_op jit(solution)/shard_map/dot_general | solution.py:244
  215.3 1.3 copy.86
  (289 shorter events, 35.1 us)
Async XLA Ops:
  0.6 90.7 %copy-start = (bf16[3,512,512]{2,1,0:T(8,128)(2,1)S(1)}, bf16[3,512,512]{2,1,0:T(8,128)(2,1)}, u32[]{:S(2)}) copy-start(bf16[3,512,512]{2,1,0:T(8,128)(2,1)} %param.25) | copy-start | bytes 4718596
  5.0 35.7 %collective-permute-start.3 = (bf16[16,6,2048]{2,0,1:T(8,128)(2,1)S(1)}, bf16[16,6,2048]{2,0,1:T(8,128)(2,1)}, u32[]{:S(2)}, u32[]{:S(2)}) collective-permute-start(bf16[16,6,2048]{2,0,1:T(8,128)(2,1)S(1)} %copy.91), channel_id=1, source_target_pairs={{2,0},{3,1},{4,2},{5,3},{6,4},{7,5},{8,6},{9,7},{10,8},{11,9},{12,... | collective-permute-start | bytes 1179656 | tf_op jit(solution)/shard_map/ppermute | solution.py:17
  6.3 33.3 %collective-permute-start.2 = (bf16[16,6,2048]{2,0,1:T(8,128)(2,1)S(1)}, bf16[16,6,2048]{2,0,1:T(8,128)(2,1)}, u32[]{:S(2)}, u32[]{:S(2)}) collective-permute-start(bf16[16,6,2048]{2,0,1:T(8,128)(2,1)S(1)} %copy.91), channel_id=1, source_target_pairs={{1,0},{2,1},{3,2},{4,3},{5,4},{6,5},{7,6},{8,7},{9,8},{10,9},{11,1... | collective-permute-start | bytes 1179656 | tf_op jit(solution)/shard_map/ppermute | solution.py:17
  11.5 26.9 %collective-permute-start.1 = (bf16[16,6,2048]{2,0,1:T(8,128)(2,1)S(1)}, bf16[16,6,2048]{2,0,1:T(8,128)(2,1)}, u32[]{:S(2)}, u32[]{:S(2)}) collective-permute-start(bf16[16,6,2048]{2,0,1:T(8,128)(2,1)S(1)} %copy.91), channel_id=1, source_target_pairs={{0,1},{1,2},{2,3},{3,4},{4,5},{5,6},{6,7},{7,8},{8,9},{9,10},{10,1... | collective-permute-start | bytes 1179656 | tf_op jit(solution)/shard_map/ppermute | solution.py:17
  17.2 20.2 %collective-permute-start = (bf16[16,6,2048]{2,0,1:T(8,128)(2,1)S(1)}, bf16[16,6,2048]{2,0,1:T(8,128)(2,1)}, u32[]{:S(2)}, u32[]{:S(2)}) collective-permute-start(bf16[16,6,2048]{2,0,1:T(8,128)(2,1)S(1)} %copy.91), channel_id=1, source_target_pairs={{0,2},{1,3},{2,4},{3,5},{4,6},{5,7},{6,8},{7,9},{8,10},{9,11},{10,... | collective-permute-start | bytes 1179656 | tf_op jit(solution)/shard_map/ppermute | solution.py:17
  55.4 29.6 %copy-start.8 = (bf16[16,32,512]{2,1,0:T(8,128)(2,1)S(1)}, bf16[16,32,512]{2,1,0:T(8,128)(2,1)}, u32[]{:S(2)}) copy-start(bf16[16,32,512]{2,1,0:T(8,128)(2,1)} %param.17) | copy-start | bytes 1572868
  55.5 29.6 %copy-start.16 = (f32[32]{0:T(128)S(1)}, f32[32]{0:T(128)}, u32[]{:S(2)}) copy-start(f32[32]{0:T(128)} %param.21) | copy-start | bytes 388
  55.5 31.3 %copy-start.13 = (bf16[512,64,1]{1,0,2:T(8,128)(2,1)S(1)}, bf16[512,64,1]{1,0,2:T(8,128)(2,1)}, u32[]{:S(2)}) copy-start(bf16[512,64,1]{1,0,2:T(8,128)(2,1)} %constant.691) | copy-start | bytes 196612
  55.5 31.3 %copy-start.14 = (bf16[32,512]{1,0:T(8,128)(2,1)S(1)}, bf16[32,512]{1,0:T(8,128)(2,1)}, u32[]{:S(2)}) copy-start(bf16[32,512]{1,0:T(8,128)(2,1)} %param.23) | copy-start | bytes 98308
  56.4 1.9 copy-start.3
  65.5 2.6 %copy-start.10 = (f32[2,8,32,512]{3,2,1,0:T(8,128)S(1)}, f32[2,8,32,512]{3,2,1,0:T(8,128)}, u32[]{:S(2)}) copy-start(f32[2,8,32,512]{3,2,1,0:T(8,128)} %get-tuple-element.720) | copy-start | bytes 3145732 | tf_op jit(solution)/shard_map/while
  69.4 1.0 copy-start.11
  71.1 1.9 copy-start.3
  80.2 2.6 %copy-start.10 = (f32[2,8,32,512]{3,2,1,0:T(8,128)S(1)}, f32[2,8,32,512]{3,2,1,0:T(8,128)}, u32[]{:S(2)}) copy-start(f32[2,8,32,512]{3,2,1,0:T(8,128)} %get-tuple-element.720) | copy-start | bytes 3145732 | tf_op jit(solution)/shard_map/while
  84.1 1.0 copy-start.11
  85.1 6.2 %copy-start.17 = (f32[512]{0:T(512)S(1)}, f32[512]{0:T(512)}, u32[]{:S(2)}) copy-start(f32[512]{0:T(512)} %param.24) | copy-start | bytes 6148
  86.8 6.4 %copy-start.9 = (bf16[16,32,512]{2,1,0:T(8,128)(2,1)}, bf16[16,32,512]{2,1,0:T(8,128)(2,1)S(1)}, u32[]{:S(2)}) copy-start(bf16[16,32,512]{2,1,0:T(8,128)(2,1)S(1)} %multiply_convert_fusion.1) | copy-start | bytes 1572868
  91.3 4.7 %copy-start.5 = (f32[1024,512]{1,0:T(8,128)}, f32[1024,512]{1,0:T(8,128)S(1)}, u32[]{:S(2)}) copy-start(f32[1024,512]{1,0:T(8,128)S(1)} %get-tuple-element.396) | copy-start | bytes 6291460
  91.3 5.2 %copy-start.15 = (s32[16]{0:T(128)S(1)}, s32[16]{0:T(128)}, u32[]{:S(2)}) copy-start(s32[16]{0:T(128)} %param.18) | copy-start | bytes 196
  93.2 1.6 copy-start.4
  95.9 30.6 %collective-permute-start.4 = (bf16[2,512,512]{1,2,0:T(8,128)(2,1)}, bf16[2,512,512]{1,2,0:T(8,128)(2,1)}, u32[]{:S(2)}, u32[]{:S(2)}) collective-permute-start(bf16[2,512,512]{1,2,0:T(8,128)(2,1)} %get-tuple-element.393), channel_id=1, source_target_pairs={{0,1},{1,2},{2,3},{3,4},{4,5},{5,6},{6,7},{7,8},{8,9},{9,10},{10,1... | collective-permute-start | bytes 3145736 | tf_op jit(solution)/shard_map/ppermute | solution.py:22
  95.9 30.6 %collective-permute-start.5 = (bf16[2,512,512]{1,2,0:T(8,128)(2,1)S(1)}, bf16[2,512,512]{1,2,0:T(8,128)(2,1)}, u32[]{:S(2)}, u32[]{:S(2)}) collective-permute-start(bf16[2,512,512]{1,2,0:T(8,128)(2,1)S(1)} %get-tuple-element.394), channel_id=1, source_target_pairs={{0,255},{1,0},{2,1},{3,2},{4,3},{5,4},{6,5},{7,6},{8,7},{9,8},{10,... | collective-permute-start | bytes 3145736 | tf_op jit(solution)/shard_map/ppermute | solution.py:22
  96.7 27.0 %collective-permute-start.7 = (s32[512]{0:T(512)S(1)}, s32[512]{0:T(512)S(1)}, u32[]{:S(2)}, u32[]{:S(2)}) collective-permute-start(s32[512]{0:T(512)S(1)} %slice.497), channel_id=1, source_target_pairs={{0,255},{1,0},{2,1},{3,2},{4,3},{5,4},{6,5},{7,6},{8,7},{9,8},{10,... | collective-permute-start | bytes 6152 | tf_op jit(solution)/shard_map/ppermute | solution.py:22
  101.3 22.4 %collective-permute-start.6 = (s32[512]{0:T(512)S(1)}, s32[512]{0:T(512)S(1)}, u32[]{:S(2)}, u32[]{:S(2)}) collective-permute-start(s32[512]{0:T(512)S(1)} %slice.495), channel_id=1, source_target_pairs={{0,1},{1,2},{2,3},{3,4},{4,5},{5,6},{6,7},{7,8},{8,9},{9,10},{10,1... | collective-permute-start | bytes 6152 | tf_op jit(solution)/shard_map/ppermute | solution.py:22
  101.5 25.0 %slice-start = ((bf16[3,512,1024]{1,2,0:T(8,128)(2,1)}), bf16[2,512,1024]{1,2,0:T(8,128)(2,1)S(1)}, s32[]{:S(2)}) async-start(bf16[3,512,1024]{1,2,0:T(8,128)(2,1)} %copy-done.4), calls=%async_computation | async-start | bytes 4194304 | tf_op jit(solution)/shard_map/slice | solution.py:231
  131.4 81.0 %copy-start.12 = (bf16[512,512]{1,0:T(8,128)(2,1)S(1)}, bf16[512,512]{1,0:T(8,128)(2,1)}, u32[]{:S(2)}) copy-start(bf16[512,512]{1,0:T(8,128)(2,1)} %param.26) | copy-start | bytes 1572868
  138.9 19.1 %copy-start.2 = (bf16[1,512,1024]{2,1,0:T(8,128)(2,1)S(1)}, bf16[1,512,1024]{2,1,0:T(8,128)(2,1)}, u32[]{:S(2)}) copy-start(bf16[1,512,1024]{2,1,0:T(8,128)(2,1)} %copy.105) | copy-start | bytes 3145732 | tf_op jit(solution)/shard_map/while
  158.0 12.5 %copy-start.6 = (bf16[512,2048]{1,0:T(8,128)(2,1)S(1)}, bf16[512,2048]{1,0:T(8,128)(2,1)}, u32[]{:S(2)}) copy-start(bf16[512,2048]{1,0:T(8,128)(2,1)} %get-tuple-element.742) | copy-start | bytes 6291460 | tf_op jit(solution)/shard_map/while
  170.7 1.3 copy-start.7
  179.4 19.1 %copy-start.2 = (bf16[1,512,1024]{2,1,0:T(8,128)(2,1)S(1)}, bf16[1,512,1024]{2,1,0:T(8,128)(2,1)}, u32[]{:S(2)}) copy-start(bf16[1,512,1024]{2,1,0:T(8,128)(2,1)} %copy.105) | copy-start | bytes 3145732 | tf_op jit(solution)/shard_map/while
  198.6 12.5 %copy-start.6 = (bf16[512,2048]{1,0:T(8,128)(2,1)S(1)}, bf16[512,2048]{1,0:T(8,128)(2,1)}, u32[]{:S(2)}) copy-start(bf16[512,2048]{1,0:T(8,128)(2,1)} %get-tuple-element.742) | copy-start | bytes 6291460 | tf_op jit(solution)/shard_map/while
  211.2 1.3 copy-start.7
  212.5 4.1 %copy-start.1 = (bf16[3,512,512]{2,1,0:T(8,128)(2,1)S(1)}, bf16[3,512,512]{2,1,0:T(8,128)(2,1)}, u32[]{:S(2)}) copy-start(bf16[3,512,512]{2,1,0:T(8,128)(2,1)} %param.25) | copy-start | bytes 4718596
where the time goes:
time: 218 us; the launch traced here: 217 us
  matrix products  77.4 us (36%)
  local copies, waits for them, and re-layouts  51 us (23%)
  waiting for transfers between devices  34.5 us (16%)
  other arithmetic  29.5 us (14%)
  starting transfers between devices  21.9 us (10%)
    sub x2, matrix products, per_window(): raw = jnp.where(allowed, jnp.exp(scores - row_peak), 0.0)  38.2 us
    dot_general x2, matrix products, per_window(): jnp.einsum('hqk,hdk->hdq', weights_bf, value_heads, preferred_element_typ...  24.9 us
    ppermute x4, waiting for transfers between devices, shifted(): lax.ppermute(array, axis, [(i, (i + by) % size) for i in range(size)])  22.2 us
    ppermute x4, starting transfers between devices, passed_along(): lax.ppermute(value, axis, [(source, source + steps) for source in range(f...  16.9 us
    while x52, other arithmetic  14.7 us
    ppermute x4, waiting for transfers between devices, passed_along(): lax.ppermute(value, axis, [(source, source + steps) for source in range(f...  12.3 us
    while x28, local copies, waits for them, and re-layouts  8.3 us
    slice x44, local copies, waits for them, and re-layouts, shift_lanes(): return jnp.concatenate([source[..., offset:], filler], axis=-1)  7.19 us
  transfers between devices with their start and end apart: 8, of which 2 were waited for; matrix products, arithmetic and copies ran while one was open for 4% of the time, Pallas kernels for 0%

commit v1 on v0

v1 whole, which is shorter than its diff:
```python
import functools

import jax
import jax.numpy as jnp
import numpy as np
from jax import lax
from jax.experimental import pallas as pl
from jax.experimental.pallas import tpu as pltpu
from jax.sharding import PartitionSpec as P

MESH = pl.DeviceIdType.MESH
BF = jnp.bfloat16
F32 = jnp.float32
NEG = -1e30
SLABS = (4, 6, 6)
ROWS = 144 * 16
Q_SCALE = 0.125 * 1.4426950408889634


def slab_tables():
    i, j, k, xh, yh, zh = np.meshgrid(
        np.arange(4), np.arange(6), np.arange(6), np.arange(4), np.arange(2), np.arange(2), indexing="ij"
    )
    x, y, z = (2 * xh + i - 1).ravel(), (4 * yh + j - 1).ravel(), (4 * zh + k - 1).ravel()
    inside = [(c >= 0) & (c < 8) for c in (x, y, z)]
    row = np.arange(ROWS)
    voxel_rows = np.zeros((ROWS, 512), np.float32)
    hit = inside[0] & inside[1] & inside[2]
    voxel_rows[row[hit], (64 * x + 8 * y + z)[hit]] = 1
    ghost_rows = np.zeros((ROWS, 384), np.float32)
    for face in range(6):
        axis, upper = face // 2, face % 2
        coord = (x, y, z)[axis]
        others = [c for a, c in enumerate((x, y, z)) if a != axis]
        ok = [inside[a] for a in range(3) if a != axis]
        hit = (coord == (8 if upper else -1)) & ok[0] & ok[1]
        ghost_rows[row[hit], (64 * face + 8 * others[0] + others[1])[hit]] = 1
    faces = np.zeros((512, 384), np.float32)
    cells = np.arange(64)
    high, low = cells // 8, cells % 8
    sources = [448 + cells, cells, 64 * high + 56 + low, 64 * high + low, 64 * high + 8 * low + 7, 64 * high + 8 * low]
    for face in range(6):
        faces[sources[face], 64 * face + cells] = 1
    xl, yl, zl, xh, yh, zh = [
        a.ravel()
        for a in np.meshgrid(*[np.arange(n) for n in (2, 4, 4, 4, 2, 2)], indexing="ij")
    ]
    x, y, z = 2 * xh + xl, 4 * yh + yl, 4 * zh + zl
    order = np.zeros((512, 512), np.float32)
    order[np.arange(512), 64 * x + 8 * y + z] = 1
    p, q, r = x // 2, y // 2, z // 2
    token = 32 * (p // 2) + 16 * (q // 2) + 8 * (r // 2) + 4 * (p % 2) + 2 * (q % 2) + r % 2
    pool = np.zeros((64, 512), np.float32)
    pool[token, np.arange(512)] = 0.125
    return [jnp.asarray(t, BF) for t in (voxel_rows, ghost_rows, faces, order, pool)]


def dot(a, b):
    return lax.dot_general(a, b, (((1,), (0,)), ((), ())), preferred_element_type=F32)


def dot_nt(a, b):
    return lax.dot_general(a, b, (((1,), (1,)), ((), ())), preferred_element_type=F32)


def kernel(
    n_space,
    n_chan,
    occ_ref,
    nbr_ref,
    bias_ref,
    gain_ref,
    proj_ref,
    feat_hbm,
    conv_w_hbm,
    latent_hbm,
    qkv_hbm,
    out_w_hbm,
    vox_hbm,
    ghost_hbm,
    face_hbm,
    order_hbm,
    pool_hbm,
    conv_out_ref,
    tokens_ref,
    feat,
    conv_w,
    lat,
    qkv_w,
    out_w,
    vox_t,
    ghost_t,
    face_t,
    order_t,
    pool_t,
    store,
    ghosts,
    slabs,
    block_w,
    masked_s,
    conv_s,
    pooled,
    proj_t,
    qw_t,
    vw_t,
    ow_t,
    base_t,
    mask,
    keys,
    vals,
    qry,
    att,
    load_sem,
    send_sem,
    recv_sem,
):
    count = n_space * n_chan
    me = lax.axis_index("space") * n_chan + lax.axis_index("chan")
    core = me % 2
    chip = me // 2

    def place(index):
        index = (index + count) % count
        return (index // n_chan, index % n_chan)

    barrier = pltpu.get_barrier_semaphore()
    for step in (-2, -1, 1, 2):
        pl.semaphore_signal(barrier, inc=1, device_id=place(me + step), device_id_type=MESH)

    loads = {}
    for index, (name, src, dst) in enumerate(
        (
            ("feat", feat_hbm, feat),
            ("face", face_hbm, face_t),
            ("vox", vox_hbm, vox_t),
            ("order", order_hbm, order_t),
            ("conv_w", conv_w_hbm, conv_w),
            ("ghost", ghost_hbm, ghost_t),
            ("lat", latent_hbm, lat.at[pl.ds(512, 1024)]),
            ("qkv", qkv_hbm, qkv_w),
            ("out_w", out_w_hbm, out_w),
            ("pool", pool_hbm, pool_t),
        )
    ):
        loads[name] = pltpu.make_async_copy(src, dst, load_sem.at[index])
        loads[name].start()

    def remote(src, dst, send, recv, target):
        return pltpu.make_async_remote_copy(
            src_ref=src,
            dst_ref=dst,
            send_sem=send_sem.at[send],
            recv_sem=recv_sem.at[recv],
            device_id=place(target),
            device_id_type=MESH,
        )

    loads["feat"].wait()
    for b in range(16):
        rows = pl.ds(b * 32, 32)
        block = feat[rows, :]
        feat[rows, :] = jnp.where(occ_ref[b] > 0, block, jnp.zeros_like(block))
    loads["face"].wait()
    own_faces = dot(feat[...], face_t[...]).astype(BF).reshape(16, 32, 384)
    store[pl.ds(pl.multiple_of(core * 16, 16), 16)] = own_faces
    store[pl.ds(80, 16)] = jnp.zeros((16, 32, 384), BF)

    pl.semaphore_wait(barrier, 4)
    own = store.at[pl.ds(core * 16, 16)]
    shared_slot = 4 - core
    shared_base = 2 * (chip - 1) + 4 * core
    sends = []
    for half in range(2):
        sends.append(
            remote(
                store.at[pl.ds(core * 16 + half * 8, 8)],
                store.at[pl.ds(shared_slot * 16 + half * 8, 8)],
                half,
                1 - core,
                shared_base + half,
            )
        )
    sends.append(remote(own, own, 2, 2, me + 1 - 2 * core))
    sends.append(remote(own, store.at[pl.ds(32, 16)], 3, 3, me + 2 - 4 * core))
    for copy in sends:
        copy.start()

    loads["vox"].wait()
    for g in range(2):
        block = feat[pl.ds(g * 256, 256), :]
        for i in range(4):
            part = dot_nt(vox_t[pl.ds(i * 576, 576), :], block).astype(BF)
            slabs[g, i] = part.reshape(6, 6, 16, 256)
    loads["order"].wait()
    masked_s[...] = dot_nt(feat[...], order_t[...]).astype(BF)

    loads["conv_w"].wait()
    rep_row = lax.broadcasted_iota(jnp.int32, (32, 256), 0)
    rep_lane = lax.broadcasted_iota(jnp.int32, (32, 256), 1)
    spread = (rep_lane % 32 == rep_row).astype(F32).astype(BF)

    def block_tap(tap, carry):
        wide = dot(conv_w[tap], spread).astype(BF)
        for b in range(8):
            block_w[tap, pl.ds(b * 32, 32), :] = jnp.where(rep_lane // 32 == b, wide, jnp.zeros_like(wide))
        return carry

    lax.fori_loop(0, 27, block_tap, 0)

    eye_row = lax.broadcasted_iota(jnp.int32, (512, 512), 0)
    eye_lane = lax.broadcasted_iota(jnp.int32, (512, 512), 1)
    eye = (eye_row == eye_lane).astype(F32).astype(BF)
    loads["qkv"].wait()
    loads["out_w"].wait()
    qw_t[...] = dot_nt(eye, qkv_w[0]).astype(BF)
    vw_t[...] = dot_nt(eye, qkv_w[2]).astype(BF)
    ow_t[...] = dot_nt(eye, out_w[...]).astype(BF)
    proj_tile = jnp.concatenate([proj_ref[...]] * 8, axis=0)
    proj_t[...] = dot_nt(eye, proj_tile).astype(BF)

    small_row = lax.broadcasted_iota(jnp.int32, (32, 32), 0)
    small_lane = lax.broadcasted_iota(jnp.int32, (32, 32), 1)
    bias_col = jnp.sum(jnp.where(small_row == small_lane, bias_ref[...], 0.0), axis=1, keepdims=True)

    m_row = lax.broadcasted_iota(jnp.int32, (64, 512), 0)
    m_lane = lax.broadcasted_iota(jnp.int32, (64, 512), 1)
    for b in range(16):
        half, slot = b // 8, b % 8
        level = jnp.where(occ_ref[b] > 0, 0.0, NEG)
        base = 512 if half == 0 else 0
        mask[half, pl.ds(base + slot * 64, 64), :] = jnp.where(m_row + slot * 64 == m_lane, 0.0, level)

    occ_lane = lax.broadcasted_iota(jnp.int32, (16, 256), 1) // 32
    for g in range(2):
        row = jnp.zeros((16, 256), F32)
        for b in range(8):
            row = jnp.where(occ_lane == b, occ_ref[g * 8 + b].astype(F32), row)
        pooled[1 + g, pl.ds(64, 16), :] = row.astype(BF)

    for h in range(8):
        vals[h, pl.ds(64, 16), :] = jnp.ones((16, 2048), BF)
        qry[h, pl.ds(64 * (1 - h % 2), 64), :] = jnp.zeros((64, 1024), BF)

    loads["ghost"].wait()
    loads["pool"].wait()
    loads["lat"].wait()

    forwards = []
    for index, slot in ((0, 3), (1, 4)):
        part = store.at[pl.ds(slot * 16 + core * 8, 8)]
        remote(part, part, 4 + index, index, me + 1 - 2 * core).wait_recv()
        forward = remote(part, part, 4 + index, 4 + index, me + 1 - 2 * core)
        forward.start()
        forwards.append(forward)
    sends[2].wait_recv()
    sends[3].wait_recv()
    for index, slot in ((0, 3), (1, 4)):
        part = store.at[pl.ds(slot * 16 + (1 - core) * 8, 8)]
        remote(part, part, 4 + index, 4 + index, me + 1 - 2 * core).wait_recv()

    lat_sends = [
        remote(lat.at[pl.ds(512, 512)], lat.at[pl.ds(1536, 512)], 6, 6, me - 1),
        remote(lat.at[pl.ds(1024, 512)], lat.at[pl.ds(0, 512)], 7, 7, me + 1),
    ]
    for copy in lat_sends:
        copy.start()

    half_lane = lax.broadcasted_iota(jnp.int32, (32, 128), 1) < 64

    def pick(b, carry):
        for pair in range(3):
            parts = []
            for side in range(2):
                peer = nbr_ref[b, 2 * pair + side]
                rel = peer // 16 - 2 * chip
                slot = jnp.where(
                    rel == 0, 0, jnp.where(rel == 1, 1, jnp.where(rel == -1, 3, jnp.where(rel == 2, 4, 2)))
                )
                row = jnp.where(peer >= 0, slot * 16 + peer % 16, 80)
                parts.append(store[row, :, pl.ds(pair * 128, 128)])
            ghosts[pl.ds(b * 32, 32), pl.ds(pair * 128, 128)] = jnp.where(half_lane, parts[0], parts[1])
        return carry

    lax.fori_loop(0, 16, pick, 0)

    for g in range(2):
        block = ghosts[pl.ds(g * 256, 256), :]
        for i in range(4):
            part = dot_nt(ghost_t[pl.ds(i * 576, 576), :], block).astype(BF)
            slabs[g, i] = slabs[g, i] + part.reshape(6, 6, 16, 256)

    def conv_group(g, carry):
        total = jnp.zeros((256, 512), F32)
        for tap in range(27):
            i, j, k = tap // 9, tap // 3 % 3, tap % 3
            patch = slabs[g, pl.ds(i, 2), pl.ds(j, 4), pl.ds(k, 4)].reshape(512, 256)
            total = total + dot_nt(block_w[tap], patch)
        rows = pl.ds(pl.multiple_of(g * 256, 256), 256)
        conv_s[rows, :] = total
        return carry

    lax.fori_loop(0, 2, conv_group, 0)
    for g in range(2):
        parts = []
        for b in range(8):
            rows = pl.ds(g * 256 + b * 32, 32)
            pre = conv_s[rows, :] + bias_col
            mixed = masked_s[rows, :].astype(F32) + pre / (1.0 + jnp.exp(-pre))
            parts.append(jnp.where(occ_ref[g * 8 + b] > 0, mixed, 0.0).astype(BF))
        conv_g = jnp.concatenate(parts, axis=0)
        pooled[1 + g, pl.ds(0, 64), :] = dot_nt(pool_t[...], conv_g).astype(BF)
        masked_s[pl.ds(g * 256, 256), :] = conv_g

    pool_sends = [
        remote(pooled.at[1], pooled.at[3], 8, 8, me - 1),
        remote(pooled.at[2], pooled.at[0], 9, 9, me + 1),
    ]
    for copy in pool_sends:
        copy.start()
    conv_out_ref[...] = dot(masked_s[...], order_t[...]).astype(BF)

    wide_row = lax.broadcasted_iota(jnp.int32, (512, 256), 0)
    wide_lane = lax.broadcasted_iota(jnp.int32, (512, 256), 1)
    same_brick = wide_row // 64 == wide_lane // 32
    first_lane = same_brick & (wide_lane % 32 == 0)
    for g in (1, 2, 0, 3):
        if g == 0:
            lat_sends[0].wait_recv()
            lat_sends[1].wait_recv()
            pool_sends[0].wait_recv()
            pool_sends[1].wait_recv()
        cells = pooled[g, pl.ds(0, 64), :]
        tall = jnp.concatenate([cells] * 8, axis=0)
        tall = jnp.where(same_brick, tall, jnp.zeros_like(tall))
        latent = lat[pl.ds(g * 512, 512), :]
        mixed = latent.astype(F32) + dot(tall, proj_tile)
        scale = lax.rsqrt(jnp.mean(mixed * mixed, axis=-1, keepdims=True) + 1e-06)
        normed = (mixed * scale * gain_ref[...]).astype(BF)
        k_all = dot(normed, qkv_w[1]).astype(BF)
        for pair in range(4):
            keys[pair, pl.ds(g * 512, 512), :] = k_all[:, pair * 128 : pair * 128 + 128]
        v_all = dot_nt(vw_t[...], normed).astype(BF)
        for h in range(8):
            vals[h, pl.ds(0, 64), pl.ds(g * 512, 512)] = v_all[h * 64 : h * 64 + 64]
        if g in (1, 2):
            lanes = pl.ds((g - 1) * 512, 512)
            q_all = (dot_nt(qw_t[...], normed) * Q_SCALE).astype(BF)
            for h in range(8):
                qry[h, pl.ds(64 * (h % 2), 64), lanes] = q_all[h * 64 : h * 64 + 64]
            base_t[:, lanes] = dot_nt(eye, latent) + dot_nt(proj_t[...], tall)
        else:
            alive = jnp.broadcast_to(pooled[g, pl.ds(64, 16), :][:1], (128, 256))
            level = dot_nt(first_lane.astype(F32).astype(BF), alive)
            level = jnp.where(level > 0.5, 0.0, NEG)
            half, start = (0, 0) if g == 0 else (1, 512)
            mask[half, pl.ds(start, 512), :] = jnp.concatenate([level] * 4, axis=1)

    for half in range(2):

        def pair_step(pair, carry):
            k_pair = keys[pair, pl.ds(half * 1024, 1024), :]
            for side in range(2):
                h = pair * 2 + side
                scores = dot(k_pair, qry[h, :, pl.ds(half * 512, 512)]) + mask[half]
                peak = jnp.max(scores, axis=0, keepdims=True)
                weights = jnp.exp2(scores - peak).astype(BF)
                out = dot(vals[h, :, pl.ds(half * 1024, 1024)], weights)
                out = (out[:64] / out[64:65]).astype(BF)
                att[pl.ds(pl.multiple_of(h * 64, 64), 64), pl.ds(half * 512, 512)] = out
            return carry

        lax.fori_loop(0, 4, pair_step, 0)
        lanes = pl.ds(half * 512, 512)
        tokens_ref[:, lanes] = (base_t[:, lanes] + dot(ow_t[...], att[:, lanes])).astype(BF)

    for copy in sends + forwards + lat_sends + pool_sends:
        copy.wait_send()


def local(n_space, n_chan, features, occupancy, neighbours, conv_weight, conv_bias, latent, token_proj, norm_gain, qkv_weight, out_weight):
    tables = slab_tables()
    smem = pl.BlockSpec(memory_space=pltpu.SMEM)
    vmem = pl.BlockSpec(memory_space=pltpu.VMEM)
    hbm = pl.BlockSpec(memory_space=pl.ANY)
    conv_out, tokens_out = pl.pallas_call(
        functools.partial(kernel, n_space, n_chan),
        out_shape=(jax.ShapeDtypeStruct((512, 512), BF), jax.ShapeDtypeStruct((512, 1024), BF)),
        in_specs=[smem, smem, vmem, vmem, vmem] + [hbm] * 10,
        out_specs=(vmem, vmem),
        scratch_shapes=[
            pltpu.VMEM((512, 512), BF),
            pltpu.VMEM((27, 32, 32), BF),
            pltpu.VMEM((2048, 512), BF),
            pltpu.VMEM((3, 512, 512), BF),
            pltpu.VMEM((512, 512), BF),
            pltpu.VMEM((ROWS, 512), BF),
            pltpu.VMEM((ROWS, 384), BF),
            pltpu.VMEM((512, 384), BF),
            pltpu.VMEM((512, 512), BF),
            pltpu.VMEM((64, 512), BF),
            pltpu.VMEM((96, 32, 384), BF),
            pltpu.VMEM((512, 384), BF),
            pltpu.VMEM((2,) + SLABS + (16, 256), BF),
            pltpu.VMEM((27, 256, 256), BF),
            pltpu.VMEM((512, 512), BF),
            pltpu.VMEM((512, 512), F32),
            pltpu.VMEM((4, 80, 256), BF),
            pltpu.VMEM((512, 256), BF),
            pltpu.VMEM((512, 512), BF),
            pltpu.VMEM((512, 512), BF),
            pltpu.VMEM((512, 512), BF),
            pltpu.VMEM((512, 1024), F32),
            pltpu.VMEM((2, 1024, 512), F32),
            pltpu.VMEM((4, 2048, 128), BF),
            pltpu.VMEM((8, 80, 2048), BF),
            pltpu.VMEM((8, 128, 1024), BF),
            pltpu.VMEM((512, 1024), BF),
            pltpu.SemaphoreType.DMA((10,)),
            pltpu.SemaphoreType.DMA((10,)),
            pltpu.SemaphoreType.DMA((10,)),
        ],
        compiler_params=pltpu.CompilerParams(
            collective_id=0, has_side_effects=True, vmem_limit_bytes=60 * 1024 * 1024
        ),
        cost_estimate=pl.CostEstimate(flops=8 * 10**9, bytes_accessed=12 * 10**6, transcendentals=9 * 10**6),
    )(
        occupancy,
        neighbours,
        conv_bias.reshape(1, 32),
        norm_gain.reshape(1, 512),
        token_proj,
        features.reshape(512, 512),
        conv_weight,
        latent,
        qkv_weight,
        out_weight,
        *tables,
    )
    return conv_out.reshape(16, 32, 512), tokens_out


def solution(mesh):
    both = ("space", "chan")
    return jax.shard_map(
        functools.partial(local, mesh.shape["space"], mesh.shape["chan"]),
        mesh=mesh,
        in_specs=(
            P(both, None, None),
            P(both),
            P(both, None),
            P(),
            P(),
            P(both, None),
            P(),
            P(),
            P(),
            P(),
        ),
        out_specs=(P(both, None, None), P(None, both)),
        check_vma=False,
    )
```

time: 218 us -> 63.6 us (0.29)
  matrix products: 77.4 us -> 0 us
  Pallas kernels: 0 us -> 57.5 us
  local copies, waits for them, and re-layouts: 51 us -> 4.3 us
  waiting for transfers between devices: 34.5 us -> 0 us
  other arithmetic: 29.5 us -> 0 us
  starting transfers between devices: 21.9 us -> 0 us
    pallas_call x0 -> x1, Pallas kernels: none -> 57.5 us  [local(): pl.pallas_call(functools.partial(kernel, n_space, n_chan), out_shape=(jax...]
    dot_general x9 -> x0, matrix products: 39.2 us -> none  [the longest x2 24.9 us: per_window(): jnp.einsum('hqk,hdk->hdq', weights_bf, value_heads, preferred_element_typ...]
    sub x2 -> x0, matrix products: 38.2 us -> none  [per_window(): raw = jnp.where(allowed, jnp.exp(scores - row_peak), 0.0)]
    ppermute x8 -> x0, waiting for transfers between devices: 34.5 us -> none  [the longest x4 22.2 us: shifted(): lax.ppermute(array, axis, [(i, (i + by) % size) for i in range(size)])]
    ppermute x8 -> x0, starting transfers between devices: 21.9 us -> none  [the longest x4 16.9 us: passed_along(): lax.ppermute(value, axis, [(source, source + steps) for source in range(f...]
    while x52 -> x0, other arithmetic: 14.7 us -> none
    slice x52 -> x0, local copies, waits for them, and re-layouts: 11.9 us -> none  [the longest x44 7.19 us: shift_lanes(): return jnp.concatenate([source[..., offset:], filler], axis=-1)]
    while x28 -> x0, local copies, waits for them, and re-layouts: 8.3 us -> none
  transfers between devices with their start and end apart: 8 -> 0, of which waited for: 2 -> 0; matrix products, arithmetic and copies ran while one was open for 4% -> 0% of each run, Pallas kernels for 0% -> 0%
where the time goes in v1:
time: 63.6 us; the launch traced here: 62.5 us
  Pallas kernels  57.5 us (90%)
  local copies, waits for them, and re-layouts  4.3 us (7%)
  between operations  0.65 us (1%)
    pallas_call x1, Pallas kernels, local(): pl.pallas_call(functools.partial(kernel, n_space, n_chan), out_shape=(jax...  57.5 us
    unnamed x5, local copies, waits for them, and re-layouts  4.3 us

profile of v1, /device:TPU:1, one launch (start us, length us, event | category | flops | bytes accessed | tf_op | source)
XLA Modules:
  0.0 62.5 jit_solution(8992540047508631255)
XLA Ops:
  0.6 1.4 %copy.17.nbr_ref = s32[16,6]{1,0:T(8,128)} copy(s32[16,6]{0,1:T(8,128)} %param.17) | data formatting | bytes 768 | tf_op args[2]
  2.0 57.5 %shard_map.158 = (bf16[512,512]{1,0:T(8,128)(2,1)}, bf16[512,1024]{1,0:T(8,128)(2,1)}) custom-call(s32[16]{0:T(128)} %occ_ref.1, s32[16,6]{1,0:T(8,128)} %copy.17.nbr_ref, f32[1,32]{1,0:T(1,128)} %bitcast.7, f32[1,512]{1,0:T(1,128)} %bitcast.6, bf16[32,512]{1,0:T(8,128)(2,1)} %proj_ref.1, bf16[512,512]{1,0:T(8,128)(2,1)} %bitcast.5, ...), custom_call_target="tpu_custom_call" | custom-call | flops 8000000000 | bytes 12000000 | tf_op jit(solution)/shard_map/pallas_call | solution.py:385
  59.5 0.0 copy-start
  59.5 2.0 %copy.20 = bf16[16,32,512]{2,1,0:T(8,128)(2,1)} copy(bf16[16,32,512]{2,1,0:T(8,128)(2,1)} %bitcast.4) | data formatting | bytes 1048576
  61.5 0.0 copy-done
  61.5 1.0 %copy.21 = bf16[512,1024]{1,0:T(8,128)(2,1)} copy(bf16[512,1024]{1,0:T(8,128)(2,1)S(1)} %copy-done) | data formatting | bytes 2097152
Async XLA Ops:
  59.5 2.0 %copy-start = (bf16[512,1024]{1,0:T(8,128)(2,1)S(1)}, bf16[512,1024]{1,0:T(8,128)(2,1)}, u32[]{:S(2)}) copy-start(bf16[512,1024]{1,0:T(8,128)(2,1)} %get-tuple-element.9) | copy-start | bytes 3145732

commit v2 on v1

--- a/solution.py
+++ b/solution.py
@@ -110,6 +110,9 @@
     vals,
     qry,
     att,
+    even_s,
+    odd_s,
+    parts_s,
     load_sem,
     send_sem,
     recv_sem,
@@ -227,8 +230,7 @@
     for b in range(16):
         half, slot = b // 8, b % 8
         level = jnp.where(occ_ref[b] > 0, 0.0, NEG)
-        base = 512 if half == 0 else 0
-        mask[half, pl.ds(base + slot * 64, 64), :] = jnp.where(m_row + slot * 64 == m_lane, 0.0, level)
+        mask[0, half, pl.ds(slot * 64, 64), :] = jnp.where(m_row + slot * 64 == m_lane, 0.0, level)
 
     occ_lane = lax.broadcasted_iota(jnp.int32, (16, 256), 1) // 32
     for g in range(2):
@@ -271,7 +273,7 @@
         for pair in range(3):
             parts = []
             for side in range(2):
-                peer = nbr_ref[b, 2 * pair + side]
+                peer = nbr_ref[2 * pair + side, b]
                 rel = peer // 16 - 2 * chip
                 slot = jnp.where(
                     rel == 0, 0, jnp.where(rel == 1, 1, jnp.where(rel == -1, 3, jnp.where(rel == 2, 4, 2)))
@@ -323,12 +325,7 @@
     wide_lane = lax.broadcasted_iota(jnp.int32, (512, 256), 1)
     same_brick = wide_row // 64 == wide_lane // 32
     first_lane = same_brick & (wide_lane % 32 == 0)
-    for g in (1, 2, 0, 3):
-        if g == 0:
-            lat_sends[0].wait_recv()
-            lat_sends[1].wait_recv()
-            pool_sends[0].wait_recv()
-            pool_sends[1].wait_recv()
+    def project(g):
         cells = pooled[g, pl.ds(0, 64), :]
         tall = jnp.concatenate([cells] * 8, axis=0)
         tall = jnp.where(same_brick, tall, jnp.zeros_like(tall))
@@ -352,26 +349,66 @@
             alive = jnp.broadcast_to(pooled[g, pl.ds(64, 16), :][:1], (128, 256))
             level = dot_nt(first_lane.astype(F32).astype(BF), alive)
             level = jnp.where(level > 0.5, 0.0, NEG)
-            half, start = (0, 0) if g == 0 else (1, 512)
-            mask[half, pl.ds(start, 512), :] = jnp.concatenate([level] * 4, axis=1)
-
-    for half in range(2):
-
-        def pair_step(pair, carry):
-            k_pair = keys[pair, pl.ds(half * 1024, 1024), :]
-            for side in range(2):
-                h = pair * 2 + side
-                scores = dot(k_pair, qry[h, :, pl.ds(half * 512, 512)]) + mask[half]
-                peak = jnp.max(scores, axis=0, keepdims=True)
-                weights = jnp.exp2(scores - peak).astype(BF)
-                out = dot(vals[h, :, pl.ds(half * 1024, 1024)], weights)
-                out = (out[:64] / out[64:65]).astype(BF)
-                att[pl.ds(pl.multiple_of(h * 64, 64), 64), pl.ds(half * 512, 512)] = out
-            return carry
-
-        lax.fori_loop(0, 4, pair_step, 0)
+            mask[1, g // 3] = jnp.concatenate([level] * 4, axis=1)
+
+    def score_chunk(side, half, pair, h, chunk, dst):
+        rows = pl.ds(chunk * 256, 256)
+        base = 512 + half * 512 if side == 0 else half * 1536
+        part = dot(keys[pair, pl.ds(base + chunk * 256, 256), :], qry[h, :, pl.ds(half * 512, 512)])
+        part = part + mask[side, half, rows, :]
+        dst[rows, :] = part
+        return jnp.max(part.reshape(32, 8, 512), axis=0)
+
+    def head_step(side, half, h, now, peaks, nxt, n_half, n_pair, n_head):
         lanes = pl.ds(half * 512, 512)
-        tokens_ref[:, lanes] = (base_t[:, lanes] + dot(ow_t[...], att[:, lanes])).astype(BF)
+        base = 512 + half * 512 if side == 0 else half * 1536
+        peak = jnp.max(peaks, axis=0, keepdims=True)
+        if side == 1:
+            own_peak = parts_s[h, pl.ds(72, 8), lanes][:1]
+            peak = jnp.maximum(peak, own_peak)
+        new_peaks, total = None, None
+        for chunk in range(2):
+            if nxt is not None:
+                top = score_chunk(side, n_half, n_pair, n_head, chunk, nxt)
+                new_peaks = top if chunk == 0 else jnp.maximum(new_peaks, top)
+            weights = jnp.exp2(now[pl.ds(chunk * 256, 256), :] - peak).astype(BF)
+            part = dot(vals[h, :, pl.ds(base + chunk * 256, 256)], weights)
+            total = part if chunk == 0 else total + part
+        if side == 0:
+            parts_s[h, pl.ds(0, 72), lanes] = total[:72]
+            parts_s[h, pl.ds(72, 8), lanes] = jnp.broadcast_to(peak, (8, 512))
+        else:
+            total = total[:72] + parts_s[h, pl.ds(0, 72), lanes] * jnp.exp2(own_peak - peak)
+            out = (total[:64] / total[64:65]).astype(BF)
+            att[pl.ds(pl.multiple_of(h * 64, 64), 64), lanes] = out
+        return new_peaks
+
+    def attend(side):
+        peaks = None
+        for chunk in range(2):
+            top = score_chunk(side, 0, 0, 0, chunk, even_s)
+            peaks = top if chunk == 0 else jnp.maximum(peaks, top)
+        for half in range(2):
+
+            def pair_step(pair, tops):
+                tops = head_step(side, half, pair * 2, even_s, tops, odd_s, half, pair, pair * 2 + 1)
+                return head_step(side, half, pair * 2 + 1, odd_s, tops, even_s, half, pair + 1, pair * 2 + 2)
+
+            peaks = lax.fori_loop(0, 3, pair_step, peaks)
+            peaks = head_step(side, half, 6, even_s, peaks, odd_s, half, 3, 7)
+            peaks = head_step(side, half, 7, odd_s, peaks, even_s if half == 0 else None, 1, 0, 0)
+            if side == 1:
+                lanes = pl.ds(half * 512, 512)
+                tokens_ref[:, lanes] = (base_t[:, lanes] + dot(ow_t[...], att[:, lanes])).astype(BF)
+
+    project(1)
+    project(2)
+    attend(0)
+    for copy in lat_sends + pool_sends:
+        copy.wait_recv()
+    project(0)
+    project(3)
+    attend(1)
 
     for copy in sends + forwards + lat_sends + pool_sends:
         copy.wait_send()
@@ -384,7 +421,7 @@
     hbm = pl.BlockSpec(memory_space=pl.ANY)
     conv_out, tokens_out = pl.pallas_call(
         functools.partial(kernel, n_space, n_chan),
-        out_shape=(jax.ShapeDtypeStruct((512, 512), BF), jax.ShapeDtypeStruct((512, 1024), BF)),
+        out_shape=(pltpu.VMEM((512, 512), BF), pltpu.VMEM((512, 1024), BF)),
         in_specs=[smem, smem, vmem, vmem, vmem] + [hbm] * 10,
         out_specs=(vmem, vmem),
         scratch_shapes=[
@@ -410,11 +447,14 @@
             pltpu.VMEM((512, 512), BF),
             pltpu.VMEM((512, 512), BF),
             pltpu.VMEM((512, 1024), F32),
-            pltpu.VMEM((2, 1024, 512), F32),
+            pltpu.VMEM((2, 2, 512, 512), F32),
             pltpu.VMEM((4, 2048, 128), BF),
             pltpu.VMEM((8, 80, 2048), BF),
             pltpu.VMEM((8, 128, 1024), BF),
             pltpu.VMEM((512, 1024), BF),
+            pltpu.VMEM((512, 512), F32),
+            pltpu.VMEM((512, 512), F32),
+            pltpu.VMEM((8, 80, 1024), F32),
             pltpu.SemaphoreType.DMA((10,)),
             pltpu.SemaphoreType.DMA((10,)),
             pltpu.SemaphoreType.DMA((10,)),
@@ -425,7 +465,7 @@
         cost_estimate=pl.CostEstimate(flops=8 * 10**9, bytes_accessed=12 * 10**6, transcendentals=9 * 10**6),
     )(
         occupancy,
-        neighbours,
+        neighbours.T,
         conv_bias.reshape(1, 32),
         norm_gain.reshape(1, 512),
         token_proj,

time: 63.6 us -> 51.6 us (0.81)
  the two profiles are of different devices: /device:TPU:1 before, /device:TPU:216 now
where the time goes in v2:
time: 51.6 us; the launch traced here: 51.4 us
  Pallas kernels  49 us (95%)
  local copies, waits for them, and re-layouts  1.77 us (3%)
  between operations  0.64 us (1%)
    pallas_call x1, Pallas kernels, local(): pl.pallas_call(functools.partial(kernel, n_space, n_chan), out_shape=(plt...  49 us
    unnamed x2, local copies, waits for them, and re-layouts  1.77 us

profile of v2, /device:TPU:216, one launch (start us, length us, event | category | flops | bytes accessed | tf_op | source)
XLA Modules:
  0.0 51.4 jit_solution(16787966694386641260)
XLA Ops:
  0.6 49.0 %shard_map.158 = (bf16[512,512]{1,0:T(8,128)(2,1)S(1)}, bf16[512,1024]{1,0:T(8,128)(2,1)S(1)}) custom-call(s32[16]{0:T(128)} %occ_ref.1, s32[6,16]{1,0:T(8,128)} %bitcast.7, f32[1,32]{1,0:T(1,128)} %bitcast.9, f32[1,512]{1,0:T(1,128)} %bitcast.8, bf16[32,512]{1,0:T(8,128)(2,1)} %proj_ref.1, bf16[512,512]{1,0:T(8,128)(2,1)} %bitcast.6, ...), custom_call_target="tpu_custom_call" | custom-call | flops 8000000000 | bytes 12000000 | tf_op jit(solution)/shard_map/pallas_call | solution.py:422
  49.7 0.8 %copy.19 = bf16[16,32,512]{2,1,0:T(8,128)(2,1)} copy(bf16[16,32,512]{2,1,0:T(8,128)(2,1)S(1)} %bitcast.5) | data formatting | bytes 1048576
  50.5 1.0 %copy.20 = bf16[512,1024]{1,0:T(8,128)(2,1)} copy(bf16[512,1024]{1,0:T(8,128)(2,1)S(1)} %get-tuple-element.7) | data formatting | bytes 2097152

commit v3 on v2

--- a/solution.py
+++ b/solution.py
@@ -14,7 +14,21 @@
 NEG = -1e30
 SLABS = (4, 6, 6)
 ROWS = 144 * 16
+GHOST_ROWS = 1792
+UNITS = 38
+HALF = 19
 Q_SCALE = 0.125 * 1.4426950408889634
+
+
+def shell_lane(x, y, z):
+    if x in (0, 7):
+        return (0 if x == 7 else 64) + 8 * y + z, False
+    if y in (0, 7):
+        return 128 + (0 if y == 7 else 48) + 8 * (x - 1) + z, False
+    index = 6 * (x - 1) + y - 1
+    if index < 16:
+        return 128 + (96 if z == 7 else 112) + index, False
+    return (0 if z == 7 else 20) + index - 16, True
 
 
 def slab_tables():
@@ -27,20 +41,34 @@
     voxel_rows = np.zeros((ROWS, 512), np.float32)
     hit = inside[0] & inside[1] & inside[2]
     voxel_rows[row[hit], (64 * x + 8 * y + z)[hit]] = 1
-    ghost_rows = np.zeros((ROWS, 384), np.float32)
-    for face in range(6):
-        axis, upper = face // 2, face % 2
-        coord = (x, y, z)[axis]
-        others = [c for a, c in enumerate((x, y, z)) if a != axis]
-        ok = [inside[a] for a in range(3) if a != axis]
-        hit = (coord == (8 if upper else -1)) & ok[0] & ok[1]
-        ghost_rows[row[hit], (64 * face + 8 * others[0] + others[1])[hit]] = 1
-    faces = np.zeros((512, 384), np.float32)
-    cells = np.arange(64)
-    high, low = cells // 8, cells % 8
-    sources = [448 + cells, cells, 64 * high + 56 + low, 64 * high + low, 64 * high + 8 * low + 7, 64 * high + 8 * low]
-    for face in range(6):
-        faces[sources[face], 64 * face + cells] = 1
+    ghost_rows = np.zeros((ROWS, 768), np.float32)
+    for r in range(ROWS):
+        cell = (int(x[r]), int(y[r]), int(z[r]))
+        out = [a for a in range(3) if not inside[a][r]]
+        if len(out) != 1:
+            continue
+        axis = out[0]
+        source = tuple((c % 8) if a == axis else c for a, c in enumerate(cell))
+        lane, extra = shell_lane(*source)
+        if extra:
+            ghost_rows[r, [640 + 40 * third + lane for third in range(3)]] = 1
+        else:
+            ghost_rows[r, (256, 0, 384)[axis] + lane] = 1
+    by_slab = ghost_rows.reshape(4, 6, 6, 16, 768)
+    parts = [by_slab[i, 1:5, 1:5] for i in (0, 3)] + [by_slab[:, j] for j in (0, 5)] + [by_slab[:, 1:5, k] for k in (0, 5)]
+    ghost_rows = np.concatenate([part.reshape(-1, 768) for part in parts])
+    faces = np.zeros((512, 256), np.float32)
+    extras = np.zeros((3, 512, 128), np.float32)
+    for vx, vy, vz in np.ndindex(8, 8, 8):
+        if min(vx, vy, vz) > 0 and max(vx, vy, vz) < 7:
+            continue
+        lane, extra = shell_lane(vx, vy, vz)
+        voxel = 64 * vx + 8 * vy + vz
+        if extra:
+            for third in range(3):
+                extras[third, voxel, 40 * third + lane] = 1
+        else:
+            faces[voxel, lane] = 1
     xl, yl, zl, xh, yh, zh = [
         a.ravel()
         for a in np.meshgrid(*[np.arange(n) for n in (2, 4, 4, 4, 2, 2)], indexing="ij")
@@ -52,7 +80,7 @@
     token = 32 * (p // 2) + 16 * (q // 2) + 8 * (r // 2) + 4 * (p % 2) + 2 * (q % 2) + r % 2
     pool = np.zeros((64, 512), np.float32)
     pool[token, np.arange(512)] = 0.125
-    return [jnp.asarray(t, BF) for t in (voxel_rows, ghost_rows, faces, order, pool)]
+    return [jnp.asarray(t, BF) for t in (voxel_rows, ghost_rows, faces, extras, order, pool)]
 
 
 def dot(a, b):
@@ -79,6 +107,7 @@
     vox_hbm,
     ghost_hbm,
     face_hbm,
+    extra_hbm,
     order_hbm,
     pool_hbm,
     conv_out_ref,
@@ -91,6 +120,7 @@
     vox_t,
     ghost_t,
     face_t,
+    extra_t,
     order_t,
     pool_t,
     store,
@@ -135,6 +165,7 @@
         (
             ("feat", feat_hbm, feat),
             ("face", face_hbm, face_t),
+            ("extra", extra_hbm, extra_t),
             ("vox", vox_hbm, vox_t),
             ("order", order_hbm, order_t),
             ("conv_w", conv_w_hbm, conv_w),
@@ -164,27 +195,33 @@
         block = feat[rows, :]
         feat[rows, :] = jnp.where(occ_ref[b] > 0, block, jnp.zeros_like(block))
     loads["face"].wait()
-    own_faces = dot(feat[...], face_t[...]).astype(BF).reshape(16, 32, 384)
-    store[pl.ds(pl.multiple_of(core * 16, 16), 16)] = own_faces
-    store[pl.ds(80, 16)] = jnp.zeros((16, 32, 384), BF)
+    own_start = core * UNITS
+    for tile in range(2):
+        cells = dot(feat[...], face_t[:, pl.ds(tile * 128, 128)]).astype(BF)
+        store[pl.ds(own_start + tile * 16, 16)] = cells.reshape(16, 32, 128)
+    loads["extra"].wait()
+    packed = [dot(feat[pl.ds(192 * t, 192 if t < 2 else 128), :], extra_t[t]) for t in range(3)]
+    packed = packed[0] + packed[1] + jnp.concatenate([packed[2], jnp.zeros((64, 128), F32)], axis=0)
+    store[pl.ds(own_start + 32, 6)] = packed.astype(BF).reshape(6, 32, 128)
+    store[pl.ds(5 * UNITS, UNITS)] = jnp.zeros((UNITS, 32, 128), BF)
 
     pl.semaphore_wait(barrier, 4)
-    own = store.at[pl.ds(core * 16, 16)]
+    own = store.at[pl.ds(own_start, UNITS)]
     shared_slot = 4 - core
     shared_base = 2 * (chip - 1) + 4 * core
     sends = []
     for half in range(2):
         sends.append(
             remote(
-                store.at[pl.ds(core * 16 + half * 8, 8)],
-                store.at[pl.ds(shared_slot * 16 + half * 8, 8)],
+                store.at[pl.ds(own_start + half * HALF, HALF)],
+                store.at[pl.ds(shared_slot * UNITS + half * HALF, HALF)],
                 half,
                 1 - core,
                 shared_base + half,
             )
         )
     sends.append(remote(own, own, 2, 2, me + 1 - 2 * core))
-    sends.append(remote(own, store.at[pl.ds(32, 16)], 3, 3, me + 2 - 4 * core))
+    sends.append(remote(own, store.at[pl.ds(2 * UNITS, UNITS)], 3, 3, me + 2 - 4 * core))
     for copy in sends:
         copy.start()
 
@@ -249,7 +286,7 @@
 
     forwards = []
     for index, slot in ((0, 3), (1, 4)):
-        part = store.at[pl.ds(slot * 16 + core * 8, 8)]
+        part = store.at[pl.ds(slot * UNITS + core * HALF, HALF)]
         remote(part, part, 4 + index, index, me + 1 - 2 * core).wait_recv()
         forward = remote(part, part, 4 + index, 4 + index, me + 1 - 2 * core)
         forward.start()
@@ -257,7 +294,7 @@
     sends[2].wait_recv()
     sends[3].wait_recv()
     for index, slot in ((0, 3), (1, 4)):
-        part = store.at[pl.ds(slot * 16 + (1 - core) * 8, 8)]
+        part = store.at[pl.ds(slot * UNITS + (1 - core) * HALF, HALF)]
         remote(part, part, 4 + index, 4 + index, me + 1 - 2 * core).wait_recv()
 
     lat_sends = [
@@ -267,29 +304,59 @@
     for copy in lat_sends:
         copy.start()
 
-    half_lane = lax.broadcasted_iota(jnp.int32, (32, 128), 1) < 64
+    lane = lax.broadcasted_iota(jnp.int32, (32, 128), 1)
+    low_x = lane < 64
+    low_y = (lane // 8 % 8 == 7, lane < 48)
+    low_z = ((lane % 8 == 7), ((lane < 96) & (lane % 8 == 7)) | ((lane >= 96) & (lane < 112)))
+    third = lane // 40
+    first_extra = lane % 40 < 20
 
     def pick(b, carry):
-        for pair in range(3):
-            parts = []
-            for side in range(2):
-                peer = nbr_ref[2 * pair + side, b]
-                rel = peer // 16 - 2 * chip
-                slot = jnp.where(
-                    rel == 0, 0, jnp.where(rel == 1, 1, jnp.where(rel == -1, 3, jnp.where(rel == 2, 4, 2)))
-                )
-                row = jnp.where(peer >= 0, slot * 16 + peer % 16, 80)
-                parts.append(store[row, :, pl.ds(pair * 128, 128)])
-            ghosts[pl.ds(b * 32, 32), pl.ds(pair * 128, 128)] = jnp.where(half_lane, parts[0], parts[1])
+        rows = pl.ds(b * 32, 32)
+        tiles = []
+        for face in range(6):
+            peer = nbr_ref[face, b]
+            rel = peer // 16 - 2 * chip
+            slot = jnp.where(
+                rel == 0, 0, jnp.where(rel == 1, 1, jnp.where(rel == -1, 3, jnp.where(rel == 2, 4, 2)))
+            )
+            start = jnp.where(peer >= 0, slot, 5) * UNITS
+            brick = jnp.where(peer >= 0, peer % 16, 0)
+            own_third = jnp.where(brick >= 12, 2, jnp.where(brick >= 6, 1, 0))
+            found = [store[start + brick]]
+            if face >= 2:
+                found.append(store[start + 16 + brick])
+            if face >= 4:
+                extra = store[start + 32 + brick - 6 * own_third]
+                mine = (third == own_third) & (first_extra if face == 4 else jnp.logical_not(first_extra))
+                found.append(jnp.where(mine, extra, jnp.zeros_like(extra)))
+            tiles.append(found)
+        picked = [jnp.where(low_y[t], tiles[2][t], tiles[3][t]) for t in range(2)]
+        picked.append(jnp.where(low_x, tiles[0][0], tiles[1][0]))
+        picked += [jnp.where(low_z[t], tiles[4][t], tiles[5][t]) for t in range(2)]
+        picked.append(tiles[4][2] + tiles[5][2])
+        for index, tile in enumerate(picked):
+            ghosts[rows, pl.ds(index * 128, 128)] = tile
         return carry
 
     lax.fori_loop(0, 16, pick, 0)
 
+    inner = pl.ds(1, 4)
     for g in range(2):
-        block = ghosts[pl.ds(g * 256, 256), :]
-        for i in range(4):
-            part = dot_nt(ghost_t[pl.ds(i * 576, 576), :], block).astype(BF)
-            slabs[g, i] = slabs[g, i] + part.reshape(6, 6, 16, 256)
+        rows = pl.ds(g * 256, 256)
+
+        def ghost_part(start, count, lanes):
+            return dot_nt(ghost_t[pl.ds(start, count), lanes], ghosts[rows, lanes]).astype(BF)
+
+        for index, i in enumerate((0, 3)):
+            part = ghost_part(index * 256, 256, pl.ds(256, 128)).reshape(4, 4, 16, 256)
+            slabs[g, i, inner, inner] = slabs[g, i, inner, inner] + part
+        for index, j in enumerate((0, 5)):
+            part = ghost_part(512 + index * 384, 384, pl.ds(0, 768)).reshape(4, 6, 16, 256)
+            slabs[g, :, j] = slabs[g, :, j] + part
+        for index, k in enumerate((0, 5)):
+            part = ghost_part(1280 + index * 256, 256, pl.ds(256, 512)).reshape(4, 4, 16, 256)
+            slabs[g, :, inner, k] = slabs[g, :, inner, k] + part
 
     def conv_group(g, carry):
         total = jnp.zeros((256, 512), F32)
@@ -422,7 +489,7 @@
     conv_out, tokens_out = pl.pallas_call(
         functools.partial(kernel, n_space, n_chan),
         out_shape=(pltpu.VMEM((512, 512), BF), pltpu.VMEM((512, 1024), BF)),
-        in_specs=[smem, smem, vmem, vmem, vmem] + [hbm] * 10,
+        in_specs=[smem, smem, vmem, vmem, vmem] + [hbm] * 11,
         out_specs=(vmem, vmem),
         scratch_shapes=[
             pltpu.VMEM((512, 512), BF),
@@ -431,12 +498,13 @@
             pltpu.VMEM((3, 512, 512), BF),
             pltpu.VMEM((512, 512), BF),
             pltpu.VMEM((ROWS, 512), BF),
-            pltpu.VMEM((ROWS, 384), BF),
-            pltpu.VMEM((512, 384), BF),
+            pltpu.VMEM((GHOST_ROWS, 768), BF),
+            pltpu.VMEM((512, 256), BF),
+            pltpu.VMEM((3, 512, 128), BF),
             pltpu.VMEM((512, 512), BF),
             pltpu.VMEM((64, 512), BF),
-            pltpu.VMEM((96, 32, 384), BF),
-            pltpu.VMEM((512, 384), BF),
+            pltpu.VMEM((6 * UNITS, 32, 128), BF),
+            pltpu.VMEM((512, 768), BF),
             pltpu.VMEM((2,) + SLABS + (16, 256), BF),
             pltpu.VMEM((27, 256, 256), BF),
             pltpu.VMEM((512, 512), BF),
@@ -455,7 +523,7 @@
             pltpu.VMEM((512, 512), F32),
             pltpu.VMEM((512, 512), F32),
             pltpu.VMEM((8, 80, 1024), F32),
-            pltpu.SemaphoreType.DMA((10,)),
+            pltpu.SemaphoreType.DMA((11,)),
             pltpu.SemaphoreType.DMA((10,)),
             pltpu.SemaphoreType.DMA((10,)),
         ],

time: 51.6 us -> 48.3 us (0.936)
  the two profiles are of different devices: /device:TPU:216 before, /device:TPU:1 now
where the time goes in v3:
time: 48.3 us; the launch traced here: 48.2 us
  Pallas kernels  45.8 us (95%)
  local copies, waits for them, and re-layouts  1.77 us (4%)
  between operations  0.64 us (1%)
    pallas_call x1, Pallas kernels, local(): pl.pallas_call(functools.partial(kernel, n_space, n_chan), out_shape=(plt...  45.8 us
    unnamed x2, local copies, waits for them, and re-layouts  1.77 us

profile of v3, /device:TPU:1, one launch (start us, length us, event | category | flops | bytes accessed | tf_op | source)
XLA Modules:
  0.0 48.2 jit_solution(13450771259672859258)
XLA Ops:
  0.6 45.8 %shard_map.167 = (bf16[512,512]{1,0:T(8,128)(2,1)S(1)}, bf16[512,1024]{1,0:T(8,128)(2,1)S(1)}) custom-call(s32[16]{0:T(128)} %occ_ref.1, s32[6,16]{1,0:T(8,128)} %bitcast.7, f32[1,32]{1,0:T(1,128)} %bitcast.9, f32[1,512]{1,0:T(1,128)} %bitcast.8, bf16[32,512]{1,0:T(8,128)(2,1)} %proj_ref.1, bf16[512,512]{1,0:T(8,128)(2,1)} %bitcast.6, ...), custom_call_target="tpu_custom_call" | custom-call | flops 8000000000 | bytes 12000000 | tf_op jit(solution)/shard_map/pallas_call | solution.py:489
  46.4 0.8 %copy.20 = bf16[16,32,512]{2,1,0:T(8,128)(2,1)} copy(bf16[16,32,512]{2,1,0:T(8,128)(2,1)S(1)} %bitcast.5) | data formatting | bytes 1048576
  47.2 1.0 %copy.21 = bf16[512,1024]{1,0:T(8,128)(2,1)} copy(bf16[512,1024]{1,0:T(8,128)(2,1)S(1)} %get-tuple-element.7) | data formatting | bytes 2097152

commit v4 on v3

--- a/solution.py
+++ b/solution.py
@@ -143,6 +143,12 @@
     even_s,
     odd_s,
     parts_s,
+    lat_k,
+    lat_v,
+    lat_q,
+    proj_k,
+    proj_v,
+    proj_q,
     load_sem,
     send_sem,
     recv_sem,
@@ -283,6 +289,19 @@
     loads["ghost"].wait()
     loads["pool"].wait()
     loads["lat"].wait()
+
+    gained_proj = (proj_tile.astype(F32) * gain_ref[...]).astype(BF)
+    proj_k[...] = dot(gained_proj, qkv_w[1]).astype(BF)
+    proj_v[...] = dot_nt(vw_t[...], gained_proj).astype(BF)
+    proj_q[...] = dot_nt(qw_t[...], gained_proj).astype(BF)
+    for half in range(2):
+        tokens = pl.ds(half * 512, 512)
+        latent = lat[pl.ds(512 + half * 512, 512), :]
+        gained = (latent.astype(F32) * gain_ref[...]).astype(BF)
+        lat_k[tokens, :] = dot(gained, qkv_w[1])
+        lat_v[:, tokens] = dot_nt(vw_t[...], gained)
+        lat_q[:, tokens] = dot_nt(qw_t[...], gained)
+        base_t[:, tokens] = dot_nt(eye, latent)
 
     forwards = []
     for index, slot in ((0, 3), (1, 4)):
@@ -399,24 +418,28 @@
         latent = lat[pl.ds(g * 512, 512), :]
         mixed = latent.astype(F32) + dot(tall, proj_tile)
         scale = lax.rsqrt(jnp.mean(mixed * mixed, axis=-1, keepdims=True) + 1e-06)
-        normed = (mixed * scale * gain_ref[...]).astype(BF)
-        k_all = dot(normed, qkv_w[1]).astype(BF)
-        for pair in range(4):
-            keys[pair, pl.ds(g * 512, 512), :] = k_all[:, pair * 128 : pair * 128 + 128]
-        v_all = dot_nt(vw_t[...], normed).astype(BF)
-        for h in range(8):
-            vals[h, pl.ds(0, 64), pl.ds(g * 512, 512)] = v_all[h * 64 : h * 64 + 64]
         if g in (1, 2):
             lanes = pl.ds((g - 1) * 512, 512)
-            q_all = (dot_nt(qw_t[...], normed) * Q_SCALE).astype(BF)
+            whole = base_t[:, lanes] + dot_nt(proj_t[...], tall)
+            base_t[:, lanes] = whole
+            scale_row = lax.rsqrt(jnp.mean(whole * whole, axis=0, keepdims=True) + 1e-06)
+            k_all = ((lat_k[lanes, :] + dot(tall, proj_k[...])) * scale).astype(BF)
+            v_all = ((lat_v[:, lanes] + dot_nt(proj_v[...], tall)) * scale_row).astype(BF)
+            q_all = ((lat_q[:, lanes] + dot_nt(proj_q[...], tall)) * (scale_row * Q_SCALE)).astype(BF)
             for h in range(8):
                 qry[h, pl.ds(64 * (h % 2), 64), lanes] = q_all[h * 64 : h * 64 + 64]
-            base_t[:, lanes] = dot_nt(eye, latent) + dot_nt(proj_t[...], tall)
         else:
+            normed = (mixed * scale * gain_ref[...]).astype(BF)
+            k_all = dot(normed, qkv_w[1]).astype(BF)
+            v_all = dot_nt(vw_t[...], normed).astype(BF)
             alive = jnp.broadcast_to(pooled[g, pl.ds(64, 16), :][:1], (128, 256))
             level = dot_nt(first_lane.astype(F32).astype(BF), alive)
             level = jnp.where(level > 0.5, 0.0, NEG)
             mask[1, g // 3] = jnp.concatenate([level] * 4, axis=1)
+        for pair in range(4):
+            keys[pair, pl.ds(g * 512, 512), :] = k_all[:, pair * 128 : pair * 128 + 128]
+        for h in range(8):
+            vals[h, pl.ds(0, 64), pl.ds(g * 512, 512)] = v_all[h * 64 : h * 64 + 64]
 
     def score_chunk(side, half, pair, h, chunk, dst):
         rows = pl.ds(chunk * 256, 256)
@@ -523,6 +546,12 @@
             pltpu.VMEM((512, 512), F32),
             pltpu.VMEM((512, 512), F32),
             pltpu.VMEM((8, 80, 1024), F32),
+            pltpu.VMEM((1024, 512), F32),
+            pltpu.VMEM((512, 1024), F32),
+            pltpu.VMEM((512, 1024), F32),
+            pltpu.VMEM((256, 512), BF),
+            pltpu.VMEM((512, 256), BF),
+            pltpu.VMEM((512, 256), BF),
             pltpu.SemaphoreType.DMA((11,)),
             pltpu.SemaphoreType.DMA((10,)),
             pltpu.SemaphoreType.DMA((10,)),

time: 48.3 us -> 49.7 us (1.029)
  Pallas kernels: 45.8 us -> 47.2 us
    pallas_call x1, Pallas kernels: 45.8 us -> 47.2 us  [local(): pl.pallas_call(functools.partial(kernel, n_space, n_chan), out_shape=(plt...]
where the time goes in v4:
time: 49.7 us; the launch traced here: 49.6 us
  Pallas kernels  47.2 us (95%)
  local copies, waits for them, and re-layouts  1.77 us (4%)
  between operations  0.64 us (1%)
    pallas_call x1, Pallas kernels, local(): pl.pallas_call(functools.partial(kernel, n_space, n_chan), out_shape=(plt...  47.2 us
    unnamed x2, local copies, waits for them, and re-layouts  1.77 us

profile of v4, /device:TPU:1, one launch (start us, length us, event | category | flops | bytes accessed | tf_op | source)
XLA Modules:
  0.0 49.6 jit_solution(14768024980833683082)
XLA Ops:
  0.6 47.2 %shard_map.167 = (bf16[512,512]{1,0:T(8,128)(2,1)S(1)}, bf16[512,1024]{1,0:T(8,128)(2,1)S(1)}) custom-call(s32[16]{0:T(128)} %occ_ref.1, s32[6,16]{1,0:T(8,128)} %bitcast.7, f32[1,32]{1,0:T(1,128)} %bitcast.9, f32[1,512]{1,0:T(1,128)} %bitcast.8, bf16[32,512]{1,0:T(8,128)(2,1)} %proj_ref.1, bf16[512,512]{1,0:T(8,128)(2,1)} %bitcast.6, ...), custom_call_target="tpu_custom_call" | custom-call | flops 8000000000 | bytes 12000000 | tf_op jit(solution)/shard_map/pallas_call | solution.py:512
  47.8 0.8 %copy.20 = bf16[16,32,512]{2,1,0:T(8,128)(2,1)} copy(bf16[16,32,512]{2,1,0:T(8,128)(2,1)S(1)} %bitcast.5) | data formatting | bytes 1048576
  48.6 1.0 %copy.21 = bf16[512,1024]{1,0:T(8,128)(2,1)} copy(bf16[512,1024]{1,0:T(8,128)(2,1)S(1)} %get-tuple-element.7) | data formatting | bytes 2097152

commit v5 on v4

--- a/solution.py
+++ b/solution.py
@@ -290,6 +290,14 @@
     loads["pool"].wait()
     loads["lat"].wait()
 
+    forwards = []
+    for index, slot in ((0, 3), (1, 4)):
+        part = store.at[pl.ds(slot * UNITS + core * HALF, HALF)]
+        remote(part, part, 4 + index, index, me + 1 - 2 * core).wait_recv()
+        forward = remote(part, part, 4 + index, 4 + index, me + 1 - 2 * core)
+        forward.start()
+        forwards.append(forward)
+
     gained_proj = (proj_tile.astype(F32) * gain_ref[...]).astype(BF)
     proj_k[...] = dot(gained_proj, qkv_w[1]).astype(BF)
     proj_v[...] = dot_nt(vw_t[...], gained_proj).astype(BF)
@@ -303,13 +311,6 @@
         lat_q[:, tokens] = dot_nt(qw_t[...], gained)
         base_t[:, tokens] = dot_nt(eye, latent)
 
-    forwards = []
-    for index, slot in ((0, 3), (1, 4)):
-        part = store.at[pl.ds(slot * UNITS + core * HALF, HALF)]
-        remote(part, part, 4 + index, index, me + 1 - 2 * core).wait_recv()
-        forward = remote(part, part, 4 + index, 4 + index, me + 1 - 2 * core)
-        forward.start()
-        forwards.append(forward)
     sends[2].wait_recv()
     sends[3].wait_recv()
     for index, slot in ((0, 3), (1, 4)):

time: 49.7 us -> 49.9 us (level)
  no operation moved by 1% of the time
where the time goes in v5:
time: 49.9 us; the launch traced here: 49.4 us
  Pallas kernels  47 us (94%)
  local copies, waits for them, and re-layouts  1.77 us (4%)
  between operations  0.64 us (1%)
    pallas_call x1, Pallas kernels, local(): pl.pallas_call(functools.partial(kernel, n_space, n_chan), out_shape=(plt...  47 us
    unnamed x2, local copies, waits for them, and re-layouts  1.77 us

profile of v5, /device:TPU:1, one launch (start us, length us, event | category | flops | bytes accessed | tf_op | source)
XLA Modules:
  0.0 49.4 jit_solution(74277083842749448)
XLA Ops:
  0.6 47.0 %shard_map.167 = (bf16[512,512]{1,0:T(8,128)(2,1)S(1)}, bf16[512,1024]{1,0:T(8,128)(2,1)S(1)}) custom-call(s32[16]{0:T(128)} %occ_ref.1, s32[6,16]{1,0:T(8,128)} %bitcast.7, f32[1,32]{1,0:T(1,128)} %bitcast.9, f32[1,512]{1,0:T(1,128)} %bitcast.8, bf16[32,512]{1,0:T(8,128)(2,1)} %proj_ref.1, bf16[512,512]{1,0:T(8,128)(2,1)} %bitcast.6, ...), custom_call_target="tpu_custom_call" | custom-call | flops 8000000000 | bytes 12000000 | tf_op jit(solution)/shard_map/pallas_call | solution.py:513
  47.7 0.8 %copy.20 = bf16[16,32,512]{2,1,0:T(8,128)(2,1)} copy(bf16[16,32,512]{2,1,0:T(8,128)(2,1)S(1)} %bitcast.5) | data formatting | bytes 1048576
  48.5 1.0 %copy.21 = bf16[512,1024]{1,0:T(8,128)(2,1)} copy(bf16[512,1024]{1,0:T(8,128)(2,1)S(1)} %get-tuple-element.7) | data formatting | bytes 2097152
